TPU v7x, 32 devices: a whole 2x2x4 slice. The times are simulated.
32 devices in a mesh: pool: 4 (over z), tp: 8 (over y, x, core).
Axes of the slice: x: 2, y: 2, z: 4, core: 2. Of those that a mesh axis runs over, the one named last changes fastest.
Arguments:
- tokens: bfloat16 [512, 8192], P(('pool', 'tp')), may hold values from -4 to 4
- lengths: int32 [4, 4], P('pool'), may hold values from 1 to 64, 128 in all within a row
- hit_pages: int32 [4, 4, 4], P('pool'), may hold values from 0 to 2047, as said below
- new_owner: int32 [4, 4], P('pool'), may hold values from 0 to 3, as said below
- w_query: bfloat16 [8192, 8192], P('pool', 'tp'), may hold values from -0.125 to 0.125
- w_keyval: bfloat16 [4096, 4096], P('pool', 'tp'), may hold values from -0.0625 to 0.0625
- w_out: bfloat16 [8192, 8192], P('tp', 'pool'), may hold values from -0.0625 to 0.0625
- pool_pages: bfloat16 [2048, 8, 8192], P('pool', 'tp'), may hold values from -65 to 65
Outputs:
- mixed: float32 [512, 8192], P(('pool', 'tp'))
- new_store: bfloat16 [32, 8, 8192], P('pool', 'tp')
Inputs may be any that keep to these rules, and one draw needn't show every extreme that they name: Page p of the pool lies on pool index p // 512. In every group g at most 6 of the 16 entries of hit_pages[g] lie on one pool index, and some pool index holds exactly 6 of them in every group. A page may appear more than once. `new_owner`: in every group at most 2 of its 4 pages go to one pool index, and some pool index receives exactly 2 from every group. Row g holds the lengths of the 4 requests packed in group g, in order, and sums to 128.
All inputs are finite; a program needn't handle non-finite values.
Results may differ from a plain program's by a relative error of at most 0.009.
Values may be sent and summed in bfloat16 or wider, within the bound.
A program may use at most 128 MiB of HBM per device.

v0:
```python
import math

import jax
import jax.numpy as jnp
from jax import lax
from jax.sharding import PartitionSpec as P

KVH = 8
HD = 128
PAGE = 32
REQS = 4
HITS = 4
CAPF = 6
CAPN = 2


EPSILON = 1e-06
ROPE_BASE = 1000000.0


def shortened(value):
    return jax.tree.map(lambda a: a.astype(jnp.bfloat16) if a.dtype == jnp.float32 else a, value)


def partner(value, axis, stride):
    mask = 2**stride
    pairs = [(source, source ^ mask) for source in range(lax.axis_size(axis))]
    return lax.ppermute(value, axis, pairs)


def rotate(values, positions):
    half = values.shape[-1] // 2
    steps_range = jnp.arange(half, dtype=jnp.float32)
    frequency = ROPE_BASE ** (-2.0 * steps_range / values.shape[-1])
    angles = positions.astype(jnp.float32)[:, None, None] * frequency[None, None, :]
    cosine = jnp.cos(angles)
    sine = jnp.sin(angles)
    first_half = values[..., :half]
    second_half = values[..., half:]
    return jnp.concatenate(
        [first_half * cosine - second_half * sine, second_half * cosine + first_half * sine],
        axis=-1,
    )


def slot_table(owners_row, capacity, seats):
    count_items = owners_row.shape[0]
    item_index = jnp.arange(count_items, dtype=jnp.int32)
    earlier_same = (owners_row[:, None] == owners_row[None, :]) & (
        item_index[None, :] < item_index[:, None]
    )
    slots = jnp.sum(earlier_same.astype(jnp.int32), axis=1)
    targets = owners_row * capacity + slots
    seat_index = jnp.arange(seats, dtype=jnp.int32)
    return targets[:, None] == seat_index[None, :]


def join_stack(held_new, held_cached, upper_half, other_new, other_cached):
    held_new = jnp.where(
        upper_half,
        jnp.concatenate([other_new, held_new], axis=0),
        jnp.concatenate([held_new, other_new], axis=0),
    )
    held_cached = jnp.where(
        upper_half,
        jnp.concatenate([other_cached, held_cached], axis=0),
        jnp.concatenate([held_cached, other_cached], axis=0),
    )
    return (held_new, held_cached)


def unstack_columns(held):
    return held.transpose(1, 0, 2).reshape(held.shape[1], held.shape[0] * held.shape[2])


def body(tokens, lengths, hit_pages, new_owner, w_query, w_keyval, w_out, pool_pages):
    rows_dev = tokens.shape[0]
    tp_count = lax.axis_size("tp")
    pool_count = lax.axis_size("pool")
    tp_rank = lax.axis_index("tp")
    group_rows = rows_dev * tp_count
    query_width = w_query.shape[1]
    part_width = w_keyval.shape[1] // 2
    heads_here = query_width // HD
    sharing = tp_count // KVH
    pages_here = pool_pages.shape[0]
    keyval_local = w_keyval.reshape(w_keyval.shape[0] * 2, part_width)
    pages_flat = pool_pages.reshape(pages_here, pool_pages.shape[1] * pool_pages.shape[2])
    tokens_wide = tokens.astype(jnp.float32)
    normed = (
        tokens_wide
        * lax.rsqrt(jnp.mean(tokens_wide * tokens_wide, axis=1, keepdims=True) + EPSILON)
    ).astype(jnp.bfloat16)
    slices = lax.all_to_all(normed, "pool", split_axis=1, concat_axis=0, tiled=True)
    slices = slices.reshape(pool_count, rows_dev, slices.shape[1])
    row_piece = lax.all_gather(slices, "tp", axis=1, tiled=True)
    partial_terms = jnp.concatenate(
        [
            jnp.einsum("prd,dc->prc", row_piece, w_query, preferred_element_type=jnp.float32),
            jnp.einsum("prd,dc->prc", row_piece, keyval_local, preferred_element_type=jnp.float32),
        ],
        axis=2,
    )
    projected = lax.psum_scatter(partial_terms, "pool", scatter_dimension=0, tiled=True)[0]
    lengths_row = lengths[0]
    ends_at = jnp.cumsum(lengths_row)
    starts_at = ends_at - lengths_row
    token_index = jnp.arange(group_rows, dtype=jnp.int32)
    request_ids = jnp.sum((token_index[:, None] >= ends_at[None, :]).astype(jnp.int32), axis=1)
    chosen = request_ids[:, None] == jnp.arange(REQS, dtype=jnp.int32)[None, :]
    start_of = jnp.sum(jnp.where(chosen, starts_at[None, :], 0), axis=1)
    positions = token_index - start_of + HITS * PAGE
    queries = rotate(
        projected[:, :query_width].reshape(group_rows, heads_here, HD), positions
    ).astype(jnp.bfloat16)
    keyval_part = projected[:, query_width:].astype(jnp.bfloat16)
    page_ids = hit_pages.reshape(-1)
    count_hits = page_ids.shape[0]
    placed_hits = slot_table(page_ids // pages_here, CAPF, pool_count * CAPF)
    wanted = jnp.sum(jnp.where(placed_hits, (page_ids % pages_here)[:, None], 0), axis=0)
    wanted = wanted.reshape(pool_count, CAPF)
    asked = lax.all_to_all(wanted, "pool", split_axis=0, concat_axis=0, tiled=True)
    found = jnp.take(pages_flat, asked.reshape(-1), axis=0)
    found = found.reshape(asked.shape[0], asked.shape[1], pages_flat.shape[1])
    returned = lax.all_to_all(found, "pool", split_axis=0, concat_axis=0, tiled=True)
    returned = returned.reshape(pool_count * CAPF, PAGE * part_width)
    cached_part = jnp.dot(
        placed_hits.astype(jnp.bfloat16), returned, preferred_element_type=jnp.float32
    ).astype(jnp.bfloat16)
    cached_part = cached_part.reshape(count_hits * PAGE, part_width)
    bit_count = sharing.bit_length() - 1
    held_new = keyval_part[None]
    held_cached = cached_part[None]
    for bit_number in range(bit_count):
        other_new, other_cached = (
            partner(shortened(held_new), "tp", bit_number).astype(held_new.dtype),
            partner(shortened(held_cached), "tp", bit_number).astype(held_cached.dtype),
        )
        upper_half = tp_rank // 2**bit_number % 2 == 1
        held_new, held_cached = join_stack(
            held_new, held_cached, upper_half, other_new, other_cached
        )
    new_head = unstack_columns(held_new)
    cached_head = unstack_columns(held_cached)
    new_keys = (
        rotate(new_head[:, :HD].astype(jnp.float32).reshape(group_rows, 1, HD), positions)
        .astype(jnp.bfloat16)
        .reshape(group_rows, HD)
    )
    stored_head = jnp.concatenate([new_keys, new_head[:, HD:]], axis=1)
    own_columns = lax.dynamic_slice_in_dim(
        stored_head, tp_rank % sharing * part_width, part_width, 1
    )
    page_count = group_rows // PAGE
    page_rows = own_columns.reshape(page_count, PAGE * part_width)
    placed_new = slot_table(new_owner[0], CAPN, pool_count * CAPN).astype(jnp.bfloat16)
    outgoing = jnp.dot(placed_new.T, page_rows, preferred_element_type=jnp.float32).astype(
        jnp.bfloat16
    )
    outgoing = outgoing.reshape(pool_count, CAPN, PAGE * part_width)
    new_store = lax.all_to_all(outgoing, "pool", split_axis=0, concat_axis=0, tiled=True).reshape(
        pool_count * CAPN, 1, PAGE * part_width
    )
    keys_all = jnp.concatenate([cached_head[:, :HD], new_keys], axis=0)
    values_all = jnp.concatenate([cached_head[:, HD:], new_head[:, HD:]], axis=0)
    cached_rows = count_hits * PAGE
    key_request = jnp.concatenate(
        [jnp.arange(cached_rows, dtype=jnp.int32) // (HITS * PAGE), request_ids]
    )
    key_order = jnp.concatenate([jnp.full((cached_rows,), -1, jnp.int32), token_index])
    block_rows = min(group_rows, 512)

    def attend(first_row):
        scores = jnp.einsum(
            "bhd,kd->hbk", queries, keys_all, preferred_element_type=jnp.float32
        ) / math.sqrt(HD)
        visible = (request_ids[:, None] == key_request[None, :]) & (
            key_order[None, :] <= token_index[:, None]
        )
        scores = jnp.where(visible[None], scores, -jnp.inf)
        highest = jnp.max(scores, axis=-1, keepdims=True)
        expanded = jnp.exp(scores - highest)
        weights = (expanded / jnp.sum(expanded, axis=-1, keepdims=True)).astype(jnp.bfloat16)
        blended = jnp.einsum(
            "hbk,kd->bhd", weights, values_all, preferred_element_type=jnp.float32
        ).astype(jnp.bfloat16)
        return blended.reshape(block_rows, query_width)

    attended = lax.map(
        attend, jnp.arange(group_rows // block_rows, dtype=jnp.int32) * block_rows
    ).reshape(group_rows, query_width)
    full_out = lax.all_gather(w_out, "pool", axis=1, tiled=True)
    summed = lax.psum_scatter(
        jnp.dot(attended, full_out, preferred_element_type=jnp.float32).astype(jnp.bfloat16),
        "tp",
        scatter_dimension=0,
        tiled=True,
    ).astype(jnp.float32)
    mixed = tokens_wide + summed
    return (mixed, new_store)


def solution(mesh):
    return jax.shard_map(
        body,
        mesh=mesh,
        in_specs=(
            P(("pool", "tp"), None),
            P("pool", None),
            P("pool", None, None),
            P("pool", None),
            P("pool", "tp"),
            P("pool", "tp"),
            P("tp", "pool"),
            P("pool", "tp", None),
        ),
        out_specs=(P(("pool", "tp"), None), P("pool", "tp", None)),
        check_vma=False,
    )
```

profile of v0, /device:TPU:0, one launch (start us, length us, event | category | flops | bytes accessed | tf_op | source)
XLA Modules:
  0.0 467.3 jit_solution(4990938977387293268)
XLA Ops:
  7.2 1.2 fusion.9
  8.4 1.1 fusion.10
  9.5 15.1 %all_to_all.35 = bf16[16,4,2048]{2,0,1:T(8,128)(2,1)} all-to-all(bf16[16,4,2048]{2,0,1:T(8,128)(2,1)S(1)} %bitcast.79), channel_id=1, replica_groups=mesh['pool'=4,'tp'=8] {'pool'}, dimensions={1} | all-to-all | bytes 524288 | tf_op jit(solution)/shard_map/all_to_all | solution.py:94
  24.7 0.4 reshape.423
  25.1 26.7 %all-gather.3.cloned.1.call-done = bf16[4,128,2048]{2,1,0:T(8,128)(2,1)} async-done(((bf16[4,16,2048]{2,1,0:T(8,128)(2,1)}), bf16[4,128,2048]{2,1,0:T(8,128)(2,1)}) %all-gather.3.cloned.1.call-update) | async-done | bytes 2097168 | tf_op jit(solution)/shard_map/all_gather | solution.py:96
  51.8 5.3 %fusion.1 = f32[4,128,1024]{2,1,0:T(8,128)S(1)} fusion(bf16[4,128,2048]{2,1,0:T(8,128)(2,1)} %all-gather.3.cloned.1.call-done, bf16[2048,1024]{1,0:T(8,128)(2,1)} %param.12), kind=kOutput, calls=%fused_computation.5 | convolution fusion | flops 2147483648 | bytes 8388608 | tf_op jit(solution)/shard_map/prd,dc->prc/dot_general | solution.py:99
  57.1 0.7 fusion.53
  57.9 1.7 pad_maximum_fusion
  59.7 0.7 all-gather.5.cloned.1.call-update
  60.5 0.2 convert_reduce_fusion
  60.7 0.1 select_reduce_fusion
  60.8 0.7 all_to_all.24
  61.4 4.6 all-to-all-start
  66.0 0.2 reduce-window.4
  66.2 0.1 convert_reduce_fusion.2
  66.4 5.1 %all-to-all-done = s32[4,1,6]{2,1,0:T(1,128)S(1)} async-done(((s32[4,1,6]{2,1,0:T(1,128)}), s32[4,1,6]{2,1,0:T(1,128)S(1)}, u32[]{:S(2)}, u32[]{:S(2)}) %all-to-all-start) | async-done | bytes 128 | tf_op jit(solution)/shard_map/all_to_all | solution.py:122
  71.5 0.5 broadcast.357
  72.0 0.7 reduce.3
  72.8 5.6 %gather_fusion = bf16[24,8192]{1,0:T(8,128)(2,1)S(1)} fusion(bf16[512,8192]{1,0:T(8,128)(2,1)} %bitcast.76, s32[1024]{0:T(1024)S(1)} %pad_clamp_fusion), kind=kCustom, calls=%fused_computation | custom fusion | bytes 786528 | tf_op jit(solution)/shard_map/jit(_take)/gather | solution.py:123
  78.4 0.1 gather.7
  78.6 0.9 broadcast_select_fusion
  79.5 3.5 all-to-all-start.1
  83.0 0.2 reduce-scatter.5.cloned.1.call-start
  83.2 0.2 fusion.11
  83.5 0.3 multiply_cosine_fusion
  83.8 28.8 %all-to-all-done.1 = bf16[4,6,8192]{2,1,0:T(8,128)(2,1)S(1)} async-done(((bf16[4,6,8192]{2,1,0:T(8,128)(2,1)}), bf16[4,6,8192]{2,1,0:T(8,128)(2,1)S(1)}, u32[]{:S(2)}, u32[]{:S(2)}) %all-to-all-start.1) | async-done | bytes 393248 | tf_op jit(solution)/shard_map/all_to_all | solution.py:125
  112.6 0.1 reshape.401
  112.8 0.3 convolution_convert_fusion.1
  113.1 0.1 reshape_transpose_broadcast_in_dim_reshape.3
  113.2 7.0 %reduce-scatter.3.cloned.1.call-done = f32[1,128,1280]{2,1,0:T(8,128)} async-done(((f32[4,128,1280]{2,1,0:T(8,128)}), f32[1,128,1280]{2,1,0:T(8,128)}) %reduce-scatter.3.cloned.1.call-update) | async-done | bytes 655376 | tf_op jit(solution)/shard_map/reduce_scatter | solution.py:104
  120.2 1.1 slice_bitcast_fusion
  121.3 0.1 copy.37
  121.4 1.1 bitcast_convert_fusion
  122.5 0.3 fusion.27
  122.8 0.2 fusion.49
  123.0 0.2 subtract_convert_fusion
  123.3 1.0 fusion.52
  124.3 1.4 fusion.8
  125.7 284.1 %all-gather.5.cloned.1.call-done = bf16[1024,8192]{1,0:T(8,128)(2,1)} async-done(((bf16[1024,2048]{1,0:T(8,128)(2,1)}), bf16[1024,8192]{1,0:T(8,128)(2,1)}) %all-gather.5.cloned.1.call-update) | async-done | bytes 16777232 | tf_op jit(solution)/shard_map/all_gather | solution.py:192
  409.8 9.6 %convolution_convert_fusion = bf16[128,8192]{1,0:T(8,128)(2,1)} fusion(bf16[128,1024]{0,1:T(8,128)(2,1)S(1)} %bitcast.80, bf16[1024,8192]{1,0:T(8,128)(2,1)} %all-gather.5.cloned.1.call-done), kind=kOutput, calls=%fused_computation.2 | convolution fusion | flops 2148532224 | bytes 19136512 | tf_op jit(solution)/shard_map/dot_general | solution.py:194
  419.4 0.2 convert_reduce_fusion.1
  419.6 0.1 pad_maximum_fusion.2
  419.7 0.3 convolution_convert_fusion.2
  420.0 0.1 reshape.410
  420.1 8.8 %all_to_all.36 = bf16[4,2,8192]{2,1,0:T(2,128)(2,1)S(1)} all-to-all(bf16[4,2,8192]{2,1,0:T(2,128)(2,1)S(1)} %reshape.410), channel_id=1, replica_groups=mesh['pool'=4,'tp'=8] {'pool'}, dimensions={0} | all-to-all | bytes 262144 | tf_op jit(solution)/shard_map/all_to_all | solution.py:161
  428.9 0.7 reshape.411
  429.7 29.3 %reduce-scatter.5.cloned.1.call-done = bf16[16,8192]{1,0:T(8,128)(2,1)} async-done(((bf16[128,8192]{1,0:T(8,128)(2,1)}), bf16[16,8192]{1,0:T(8,128)(2,1)}) %reduce-scatter.5.cloned.1.call-update) | async-done | bytes 262160 | tf_op jit(solution)/shard_map/reduce_scatter | solution.py:193
  459.0 1.8 convert_add_fusion
  (39 shorter events, 0.6 us)
Async XLA Ops:
  7.2 17.5 %copy-start.1 = (bf16[1024,512]{1,0:T(8,128)(2,1)S(1)}, bf16[1024,512]{1,0:T(8,128)(2,1)}, u32[]{:S(2)}) copy-start(bf16[1024,512]{1,0:T(8,128)(2,1)} %param.13) | copy-start | bytes 3145732
  7.2 44.6 %all-gather.3.cloned.1.call-start = ((), (), s32[]{:S(2)}) async-start(), calls=%async_computation.6 | async-start | bytes 2359296 | tf_op jit(solution)/shard_map/all_gather | solution.py:96
  24.7 95.5 %reduce-scatter.3.cloned.1.call-start = ((), (), s32[]{:S(2)}) async-start(), calls=%async_computation.7 | async-start | bytes 3276800 | tf_op jit(solution)/shard_map/reduce_scatter | solution.py:104
  51.8 5.3 %copy-start.4 = (bf16[4,128,2048]{2,1,0:T(8,128)(2,1)S(1)}, bf16[4,128,2048]{2,1,0:T(8,128)(2,1)}, u32[]{:S(2)}) copy-start(bf16[4,128,2048]{2,1,0:T(8,128)(2,1)} %all-gather.3.cloned.1.call-done) | copy-start | bytes 6291460
  59.6 0.8 copy-start.3
  59.6 6.4 %copy-start.5 = (s32[1,4]{1,0:T(1,128)S(1)}, s32[1,4]{1,0:T(1,128)}, u32[]{:S(2)}) copy-start(s32[1,4]{1,0:T(1,128)} %param.9) | copy-start | bytes 52
  59.6 350.1 %all-gather.5.cloned.1.call-start = ((), (), s32[]{:S(2)}) async-start(), calls=%async_computation.8 | async-start | bytes 20971520 | tf_op jit(solution)/shard_map/all_gather | solution.py:192
  61.4 10.1 %all-to-all-start = ((s32[4,1,6]{2,1,0:T(1,128)}), s32[4,1,6]{2,1,0:T(1,128)S(1)}, u32[]{:S(2)}, u32[]{:S(2)}) async-start(s32[4,1,6]{2,1,0:T(1,128)} %bitcast), calls=%async_computation | async-start | bytes 4096 | tf_op jit(solution)/shard_map/all_to_all | solution.py:122
  72.8 10.5 %copy-start.2 = (s32[640]{0:T(1024)S(1)}, s32[640]{0:T(1024)}, u32[]{:S(2)}) copy-start(s32[640]{0:T(1024)} %constant.104.clone.1) | copy-start | bytes 7684
  79.5 33.1 %all-to-all-start.1 = ((bf16[4,6,8192]{2,1,0:T(8,128)(2,1)}), bf16[4,6,8192]{2,1,0:T(8,128)(2,1)S(1)}, u32[]{:S(2)}, u32[]{:S(2)}) async-start(bf16[4,6,8192]{2,1,0:T(8,128)(2,1)} %broadcast_select_fusion), calls=%async_computation.1 | async-start | bytes 1048576 | tf_op jit(solution)/shard_map/all_to_all | solution.py:125
  83.0 376.0 %reduce-scatter.5.cloned.1.call-start = ((), (), s32[]{:S(2)}) async-start(), calls=%async_computation.9 | async-start | bytes 2359296 | tf_op jit(solution)/shard_map/reduce_scatter | solution.py:193
  409.8 9.6 %copy-start.6 = (s32[1,4]{1,0:T(1,128)S(1)}, s32[1,4]{1,0:T(1,128)}, u32[]{:S(2)}) copy-start(s32[1,4]{1,0:T(1,128)} %param.11) | copy-start | bytes 52
  419.4 39.6 %copy-start = (bf16[16,8192]{1,0:T(8,128)(2,1)S(1)}, bf16[16,8192]{1,0:T(8,128)(2,1)}, u32[]{:S(2)}) copy-start(bf16[16,8192]{1,0:T(8,128)(2,1)} %param.8) | copy-start | bytes 786436
Sparse Core Ops, SparseCore 0:
  24.8 26.9 all-gather.2
  59.7 60.4 reduce-scatter.2
  121.8 287.9 all-gather.4
  419.5 39.4 reduce-scatter.4
where the time goes:
time: 468 us; the launch traced here: 467 us
  waiting for transfers between devices  382 us (82%)
  blocking collectives  23.9 us (5%)
  matrix products  18.6 us (4%)
  between operations  14 us (3%)
  other arithmetic  10.5 us (2%)
  local copies, waits for them, and re-layouts  10.1 us (2%)
  starting transfers between devices  8.41 us (2%)
    all_gather x1, waiting for transfers between devices, body(): full_out = lax.all_gather(w_out, 'pool', axis=1, tiled=True)  284 us
    reduce_scatter x1, waiting for transfers between devices, body(): lax.psum_scatter(jnp.dot(attended, full_out, preferred_element_type=jnp.f...  29.3 us
    all_to_all x1, waiting for transfers between devices, body(): lax.all_to_all(found, 'pool', split_axis=0, concat_axis=0, tiled=True)  28.8 us
    all_gather x1, waiting for transfers between devices, body(): row_piece = lax.all_gather(slices, 'tp', axis=1, tiled=True)  26.7 us
    all_to_all x1, blocking collectives, body(): lax.all_to_all(normed, 'pool', split_axis=1, concat_axis=0, tiled=True)  15.1 us
    dot_general x1, matrix products, body(): jnp.dot(attended, full_out, preferred_element_type=jnp.float32)  9.6 us
  transfers between devices with their start and end apart: 6, of which 6 were waited for; matrix products, arithmetic and copies ran while one was open for 4% of the time, Pallas kernels for 0%

commit v1 on v0

--- a/solution.py
+++ b/solution.py
@@ -1,8 +1,11 @@
+import functools
 import math
 
 import jax
 import jax.numpy as jnp
 from jax import lax
+from jax.experimental import pallas as pl
+from jax.experimental.pallas import tpu as pltpu
 from jax.sharding import PartitionSpec as P
 
 KVH = 8
@@ -101,7 +104,9 @@
         ],
         axis=2,
     )
-    projected = lax.psum_scatter(partial_terms, "pool", scatter_dimension=0, tiled=True)[0]
+    projected = lax.psum_scatter(
+        partial_terms.astype(jnp.bfloat16), "pool", scatter_dimension=0, tiled=True
+    )[0].astype(jnp.float32)
     lengths_row = lengths[0]
     ends_at = jnp.cumsum(lengths_row)
     starts_at = ends_at - lengths_row
@@ -189,20 +194,462 @@
     attended = lax.map(
         attend, jnp.arange(group_rows // block_rows, dtype=jnp.int32) * block_rows
     ).reshape(group_rows, query_width)
-    full_out = lax.all_gather(w_out, "pool", axis=1, tiled=True)
-    summed = lax.psum_scatter(
-        jnp.dot(attended, full_out, preferred_element_type=jnp.float32).astype(jnp.bfloat16),
-        "tp",
-        scatter_dimension=0,
-        tiled=True,
-    ).astype(jnp.float32)
+    every = lax.all_gather(attended, "pool", axis=0, tiled=False)
+    parts = jnp.einsum("prd,dc->prc", every, w_out, preferred_element_type=jnp.float32)
+    scattered = lax.psum_scatter(
+        parts.astype(jnp.bfloat16), "tp", scatter_dimension=1, tiled=True
+    )
+    summed = lax.all_to_all(scattered, "pool", split_axis=0, concat_axis=2, tiled=True)
+    summed = summed.reshape(rows_dev, tokens.shape[1]).astype(jnp.float32)
     mixed = tokens_wide + summed
     return (mixed, new_store)
 
 
+MESH = pl.DeviceIdType.MESH
+VMEM_BYTES = 56 * 1024 * 1024
+CORES = 2
+
+
+def remote(source, target, send_sem, recv_sem, device):
+    return pltpu.make_async_remote_copy(
+        src_ref=source,
+        dst_ref=target,
+        send_sem=send_sem,
+        recv_sem=recv_sem,
+        device_id=device,
+        device_id_type=MESH,
+    )
+
+
+def places(pools, chips):
+    pool = lax.axis_index("pool")
+    rank = lax.axis_index("tp")
+    chip, core = rank // CORES, rank % CORES
+    pool_peers = [lax.rem(pool + k, pools) for k in range(1, pools)]
+    chip_peers = [lax.rem(chip + k, chips) for k in range(1, chips)]
+    return pool, rank, chip, core, pool_peers, chip_peers
+
+
+def meet(pool, rank, chip, core, pool_peers, chip_peers):
+    barrier = pltpu.get_barrier_semaphore()
+    devices = [(peer, rank) for peer in pool_peers]
+    devices += [(pool, peer * CORES + core) for peer in chip_peers]
+    devices += [(pool, chip * CORES + 1 - core)]
+    for device in devices:
+        pl.semaphore_signal(barrier, inc=1, device_id=device, device_id_type=MESH)
+    pl.semaphore_wait(barrier, len(devices))
+
+
+def project_kernel(
+    pools, chips, seats,
+    tokens_ref, wanted_ref, query_ref, keyval_ref, pages_ref,
+    projected_ref, fetched_ref,
+    normed, rows, weights, store, ids, numbers, page_out, page_in, part_out, part_in, own,
+    load_sem, id_send, id_recv, number_sem, pool_send, row_recv, chip_send, side_send,
+    page_send, page_recv, part_send, part_recv,
+):
+    pool, rank, chip, core, pool_peers, chip_peers = places(pools, chips)
+    depth = rows.shape[3]
+    query_width = query_ref.shape[1]
+    width = weights.shape[1]
+    page, part = page_out.shape[2:]
+    sibling = (pool, chip * CORES + 1 - core)
+    loads = [
+        pltpu.make_async_copy(pages_ref, store, load_sem.at[0]),
+        pltpu.make_async_copy(query_ref, weights.at[:, pl.ds(0, query_width)], load_sem.at[1]),
+        pltpu.make_async_copy(
+            keyval_ref, weights.at[:, pl.ds(query_width, width - query_width)], load_sem.at[2]
+        ),
+    ]
+    for load in loads:
+        load.start()
+    wide = tokens_ref[...].astype(jnp.float32)
+    scale = lax.rsqrt(jnp.mean(wide * wide, axis=1, keepdims=True) + EPSILON)
+    scaled = (wide * scale).astype(jnp.bfloat16)
+    for p in range(pools):
+        normed[p] = scaled[:, p * depth : (p + 1) * depth]
+    rows[pool, rank] = normed[pool]
+    ids[pool] = wanted_ref[pool]
+    meet(pool, rank, chip, core, pool_peers, chip_peers)
+    sends = []
+
+    def send(copy):
+        copy.start()
+        sends.append(copy)
+
+    for peer in pool_peers:
+        send(remote(wanted_ref.at[peer], ids.at[pool], id_send.at[peer], id_recv.at[pool], (peer, rank)))
+    for peer in pool_peers:
+        send(
+            remote(normed.at[peer], rows.at[pool, rank], pool_send.at[peer], row_recv.at[pool, rank], (peer, rank))
+        )
+
+    def arrived(group, source):
+        block = rows.at[group, source]
+        remote(block, block, side_send.at[group, source], row_recv.at[group, source], sibling).wait_recv()
+
+    def to_sibling(group, source):
+        block = rows.at[group, source]
+        send(remote(block, block, side_send.at[group, source], row_recv.at[group, source], sibling))
+
+    def to_chips(group):
+        block = rows.at[group, rank]
+        for peer in chip_peers:
+            send(
+                remote(
+                    block, block, chip_send.at[group, peer], row_recv.at[group, rank], (pool, peer * CORES + core)
+                )
+            )
+        to_sibling(group, rank)
+
+    to_chips(pool)
+    for peer in pool_peers:
+        arrived(peer, rank)
+        to_chips(peer)
+
+    for peer in pool_peers:
+        remote(ids.at[peer], ids.at[peer], id_send.at[peer], id_recv.at[peer], (peer, rank)).wait_recv()
+    numbers_copy = pltpu.make_async_copy(ids, numbers, number_sem)
+    numbers_copy.start()
+    numbers_copy.wait()
+    loads[0].wait()
+    block_rows = store.shape[1]
+    lane = lax.broadcasted_iota(jnp.int32, (page, page * block_rows), 1)
+    line = lax.broadcasted_iota(jnp.int32, (page, page * block_rows), 0)
+    offset = lane - line * block_rows
+
+    def fetch(group):
+        def one(seat, carry):
+            block = store[numbers[group, 0, seat]]
+            tall = jnp.concatenate([block[:, t * part : (t + 1) * part] for t in range(page)], axis=0)
+            chosen = (offset == numbers[group, 1, seat]).astype(jnp.float32).astype(jnp.bfloat16)
+            page_out[group, seat] = jnp.dot(chosen, tall, preferred_element_type=jnp.float32).astype(jnp.bfloat16)
+            return carry
+
+        lax.fori_loop(0, seats, one, 0)
+
+    def pass_on(group):
+        for peer in chip_peers:
+            arrived(group, peer * CORES + core)
+            to_sibling(group, peer * CORES + core)
+
+    def multiply(group):
+        for c in range(chips):
+            arrived(group, c * CORES + 1 - core)
+        left = rows[group].reshape(rows.shape[1] * rows.shape[2], depth)
+        return left
+
+    step = 256 if width % 256 == 0 else 128
+
+    def project(group, target, dtype):
+        left = multiply(group)
+
+        def one(c, carry):
+            columns = pl.ds(pl.multiple_of(c * step, step), step)
+            target[:, columns] = jnp.dot(left, weights[:, columns], preferred_element_type=jnp.float32).astype(dtype)
+            return carry
+
+        lax.fori_loop(0, width // step, one, 0)
+
+    pass_on(pool)
+    for index, peer in enumerate(pool_peers):
+        fetch(peer)
+        send(remote(page_out.at[peer], page_in.at[pool], page_send.at[peer], page_recv.at[pool], (peer, rank)))
+        pass_on(peer)
+        if index == 0:
+            loads[1].wait()
+            loads[2].wait()
+        project(peer, part_out.at[peer], jnp.bfloat16)
+        send(remote(part_out.at[peer], part_in.at[pool], part_send.at[peer], part_recv.at[pool], (peer, rank)))
+    project(pool, own, jnp.float32)
+    fetch(pool)
+    for peer in pool_peers:
+        remote(page_in.at[peer], page_in.at[peer], page_send.at[peer], page_recv.at[peer], (peer, rank)).wait_recv()
+    for p in range(pools):
+        fetched_ref[p] = page_in[p]
+    fetched_ref[pool] = page_out[pool]
+    for peer in pool_peers:
+        remote(part_in.at[peer], part_in.at[peer], part_send.at[peer], part_recv.at[peer], (peer, rank)).wait_recv()
+    total = own[...]
+    for peer in pool_peers:
+        total = total + part_in[peer].astype(jnp.float32)
+    projected_ref[...] = total
+    for copy in sends:
+        copy.wait_send()
+
+
+def output_kernel(
+    pools, chips, heads, halves, new_seats,
+    tokens_ref, projected_ref, fetched_ref, cosine_ref, sine_ref, request_ref, key_request_ref, placed_ref, out_ref,
+    mixed_ref, store_ref,
+    weights, keys, values, page_out, page_in, attended, parts, side_in, chip_out, chip_in, last_out, last_in,
+    load_sem, page_send, page_recv, att_send, att_recv, side_send, side_recv, chip_send, chip_recv,
+    last_send, last_recv,
+):
+    pool, rank, chip, core, pool_peers, chip_peers = places(pools, chips)
+    sibling = (pool, chip * CORES + 1 - core)
+    load = pltpu.make_async_copy(out_ref, weights, load_sem)
+    load.start()
+    group_rows = projected_ref.shape[0]
+    cached_rows = keys.shape[0] - group_rows
+    query_width = heads * HD
+    cosine, sine = cosine_ref[...], sine_ref[...]
+
+    def turned(part):
+        return part * cosine + pltpu.roll(part, HD // 2, axis=1) * sine
+
+    new_keys = projected_ref[:, query_width : query_width + HD].astype(jnp.bfloat16).astype(jnp.float32)
+    new_keys = turned(new_keys).astype(jnp.bfloat16)
+    new_values = projected_ref[:, query_width + HD :].astype(jnp.bfloat16)
+    cached = fetched_ref[...].reshape(cached_rows, 2 * HD)
+    keys[0:cached_rows] = cached[:, :HD]
+    values[0:cached_rows] = cached[:, HD:]
+    keys[cached_rows:] = new_keys
+    values[cached_rows:] = new_values
+    count = group_rows // PAGE
+    stored = jnp.concatenate([new_keys.astype(jnp.float32), new_values.astype(jnp.float32)], axis=1)
+    for seat in range(pools * new_seats):
+        total = stored[0:PAGE] * placed_ref[seat]
+        for n in range(1, count):
+            total = total + stored[n * PAGE : (n + 1) * PAGE] * placed_ref[n * pools * new_seats + seat]
+        page_out[seat // new_seats, seat % new_seats] = total.astype(jnp.bfloat16)
+    meet(pool, rank, chip, core, pool_peers, chip_peers)
+    sends = []
+
+    def send(copy):
+        copy.start()
+        sends.append(copy)
+
+    row = lax.broadcasted_iota(jnp.int32, (group_rows, keys.shape[0]), 0)
+    column = lax.broadcasted_iota(jnp.int32, (group_rows, keys.shape[0]), 1) - cached_rows
+    visible = (request_ref[...] == key_request_ref[...]) & (column <= row)
+    heads_half = heads // halves
+    for half in range(halves):
+        for h in range(heads_half):
+            first = (half * heads_half + h) * HD
+            query = turned(projected_ref[:, first : first + HD]).astype(jnp.bfloat16)
+            scores = lax.dot_general(
+                query, keys[...], (((1,), (1,)), ((), ())), preferred_element_type=jnp.float32
+            ) * (1.0 / math.sqrt(HD))
+            scores = jnp.where(visible, scores, -jnp.inf)
+            grown = jnp.exp(scores - jnp.max(scores, axis=1, keepdims=True))
+            share = (grown * (1.0 / jnp.sum(grown, axis=1, keepdims=True))).astype(jnp.bfloat16)
+            attended[pool, half, :, h * HD : (h + 1) * HD] = jnp.dot(
+                share, values[...], preferred_element_type=jnp.float32
+            ).astype(jnp.bfloat16)
+        block = attended.at[pool, half]
+        for peer in pool_peers:
+            send(remote(block, block, att_send.at[peer, half], att_recv.at[pool, half], (peer, rank)))
+    for peer in pool_peers:
+        send(remote(page_out.at[peer], page_in.at[pool], page_send.at[peer], page_recv.at[pool], (peer, rank)))
+    load.wait()
+    half_width = heads_half * HD
+    rows_dev, width = parts.shape[3:]
+    step = 512 if width % 512 == 0 else 128
+
+    def multiply(group):
+        def one(c, carry):
+            columns = pl.ds(pl.multiple_of(c * step, step), step)
+            total = jnp.dot(attended[group, 0], weights[0:half_width, columns], preferred_element_type=jnp.float32)
+            for half in range(1, halves):
+                total = total + jnp.dot(
+                    attended[group, half],
+                    weights[half * half_width : (half + 1) * half_width, columns],
+                    preferred_element_type=jnp.float32,
+                )
+            parts[group, :, :, :, columns] = total.astype(jnp.bfloat16).reshape(chips, CORES, rows_dev, step)
+            return carry
+
+        lax.fori_loop(0, width // step, one, 0)
+        send(remote(parts.at[group, :, 1 - core], side_in.at[group], side_send.at[group], side_recv.at[group], sibling))
+
+    def join_side(group):
+        remote(side_in.at[group], side_in.at[group], side_send.at[group], side_recv.at[group], sibling).wait_recv()
+        total = parts[group, :, core].astype(jnp.float32) + side_in[group].astype(jnp.float32)
+        chip_out[group] = total.astype(jnp.bfloat16)
+        for peer in chip_peers:
+            send(
+                remote(
+                    chip_out.at[group, peer], chip_in.at[group, chip],
+                    chip_send.at[group, peer], chip_recv.at[group, chip], (pool, peer * CORES + core),
+                )
+            )
+
+    def join_chips(group):
+        total = chip_out[group, chip].astype(jnp.float32)
+        for peer in chip_peers:
+            block = chip_in.at[group, peer]
+            remote(
+                block, block, chip_send.at[group, peer], chip_recv.at[group, peer], (pool, peer * CORES + core)
+            ).wait_recv()
+            total = total + chip_in[group, peer].astype(jnp.float32)
+        return total
+
+    order = [pool] + pool_peers
+    for index in range(pools + 2):
+        if index < pools:
+            group = order[index]
+            if index:
+                for half in range(halves):
+                    block = attended.at[group, half]
+                    remote(block, block, att_send.at[group, half], att_recv.at[group, half], (group, rank)).wait_recv()
+            multiply(group)
+        if 1 <= index <= pools:
+            join_side(order[index - 1])
+        if index >= 2:
+            group = order[index - 2]
+            total = join_chips(group)
+            last_out[group] = total.astype(jnp.bfloat16)
+            if index > 2:
+                send(
+                    remote(last_out.at[group], last_in.at[pool], last_send.at[group], last_recv.at[pool], (group, rank))
+                )
+    last_in[pool] = last_out[pool]
+    for peer in pool_peers:
+        remote(page_in.at[peer], page_in.at[peer], page_send.at[peer], page_recv.at[peer], (peer, rank)).wait_recv()
+    page_in[pool] = page_out[pool]
+    store_ref[...] = page_in[...].reshape(store_ref.shape)
+    for peer in pool_peers:
+        remote(last_in.at[peer], last_in.at[peer], last_send.at[peer], last_recv.at[peer], (peer, rank)).wait_recv()
+    for p in range(pools):
+        columns = slice(p * width, (p + 1) * width)
+        mixed_ref[:, columns] = tokens_ref[:, columns].astype(jnp.float32) + last_in[p].astype(jnp.float32)
+    for copy in sends:
+        copy.wait_send()
+
+
+def fused(tokens, lengths, hit_pages, new_owner, w_query, w_keyval, w_out, pool_pages):
+    rows_dev, features = tokens.shape
+    pools, ranks = lax.axis_size("pool"), lax.axis_size("tp")
+    chips = ranks // CORES
+    group_rows = rows_dev * ranks
+    query_width = w_query.shape[1]
+    heads = query_width // HD
+    part = w_keyval.shape[1] // 2
+    width = query_width + part
+    depth = w_query.shape[0]
+    pages_here = pool_pages.shape[0]
+    block_rows = 16
+    keyval = w_keyval.reshape(depth, part)
+    store = pool_pages.reshape(pages_here // block_rows, block_rows, PAGE * part)
+
+    page_ids = hit_pages.reshape(-1)
+    placed_hits = slot_table(page_ids // pages_here, CAPF, pools * CAPF)
+    local = (page_ids % pages_here)[:, None]
+    wanted = jnp.sum(jnp.where(placed_hits, local, 0), axis=0).reshape(pools, 1, CAPF)
+    wanted = jnp.concatenate([wanted // block_rows, wanted % block_rows], axis=1)
+    wanted = jnp.pad(wanted, ((0, 0), (0, 6), (0, 128 - CAPF)))
+    hit_request = jnp.arange(page_ids.shape[0], dtype=jnp.int32)[:, None] // HITS
+    seat_request = jnp.sum(jnp.where(placed_hits, hit_request + 1, 0), axis=0) - 1
+
+    lengths_row = lengths[0]
+    ends_at = jnp.cumsum(lengths_row)
+    starts_at = ends_at - lengths_row
+    token_index = jnp.arange(group_rows, dtype=jnp.int32)
+    request_ids = jnp.sum((token_index[:, None] >= ends_at[None, :]).astype(jnp.int32), axis=1)
+    chosen = request_ids[:, None] == jnp.arange(REQS, dtype=jnp.int32)[None, :]
+    start_of = jnp.sum(jnp.where(chosen, starts_at[None, :], 0), axis=1)
+    positions = token_index - start_of + HITS * PAGE
+    half = HD // 2
+    frequency = ROPE_BASE ** (-2.0 * jnp.arange(half, dtype=jnp.float32) / HD)
+    angles = positions.astype(jnp.float32)[:, None] * frequency[None, :]
+    cosine, sine = jnp.cos(angles), jnp.sin(angles)
+    cosine = jnp.concatenate([cosine, cosine], axis=1)
+    sine = jnp.concatenate([-sine, sine], axis=1)
+    key_request = jnp.concatenate([jnp.repeat(seat_request, PAGE), request_ids])[None, :]
+    placed_new = slot_table(new_owner[0], CAPN, pools * CAPN).astype(jnp.float32).reshape(-1)
+
+    vmem = pl.BlockSpec(memory_space=pltpu.VMEM)
+    smem = pl.BlockSpec(memory_space=pltpu.SMEM)
+    anywhere = pl.BlockSpec(memory_space=pl.ANY)
+    bf16, f32 = jnp.bfloat16, jnp.float32
+    dma = pltpu.SemaphoreType.DMA
+    projected, fetched = pl.pallas_call(
+        functools.partial(project_kernel, pools, chips, CAPF),
+        out_shape=(
+            jax.ShapeDtypeStruct((group_rows, width), f32),
+            jax.ShapeDtypeStruct((pools, CAPF, PAGE, part), bf16),
+        ),
+        in_specs=[vmem, vmem, anywhere, anywhere, anywhere],
+        out_specs=(vmem, vmem),
+        scratch_shapes=[
+            pltpu.VMEM((pools, rows_dev, depth), bf16),
+            pltpu.VMEM((pools, ranks, rows_dev, depth), bf16),
+            pltpu.VMEM((depth, width), bf16),
+            pltpu.VMEM(store.shape, bf16),
+            pltpu.VMEM(wanted.shape, jnp.int32),
+            pltpu.SMEM(wanted.shape, jnp.int32),
+            pltpu.VMEM((pools, CAPF, PAGE, part), bf16),
+            pltpu.VMEM((pools, CAPF, PAGE, part), bf16),
+            pltpu.VMEM((pools, group_rows, width), bf16),
+            pltpu.VMEM((pools, group_rows, width), bf16),
+            pltpu.VMEM((group_rows, width), f32),
+            dma((3,)),
+            dma((pools,)),
+            dma((pools,)),
+            dma(()),
+            dma((pools,)),
+            dma((pools, ranks)),
+            dma((pools, chips)),
+            dma((pools, ranks)),
+            dma((pools,)),
+            dma((pools,)),
+            dma((pools,)),
+            dma((pools,)),
+        ],
+        compiler_params=pltpu.CompilerParams(
+            collective_id=0, has_side_effects=True, vmem_limit_bytes=VMEM_BYTES
+        ),
+        name="project",
+    )(tokens, wanted, w_query, keyval, store)
+
+    halves = 2 if heads % 2 == 0 else 1
+    keys_count = pools * CAPF * PAGE + group_rows
+    mixed, stored = pl.pallas_call(
+        functools.partial(output_kernel, pools, chips, heads, halves, CAPN),
+        out_shape=(
+            jax.ShapeDtypeStruct((rows_dev, features), f32),
+            jax.ShapeDtypeStruct((pools * CAPN, PAGE, part), bf16),
+        ),
+        in_specs=[vmem] * 7 + [smem, anywhere],
+        out_specs=(vmem, vmem),
+        scratch_shapes=[
+            pltpu.VMEM(w_out.shape, bf16),
+            pltpu.VMEM((keys_count, HD), bf16),
+            pltpu.VMEM((keys_count, HD), bf16),
+            pltpu.VMEM((pools, CAPN, PAGE, part), bf16),
+            pltpu.VMEM((pools, CAPN, PAGE, part), bf16),
+            pltpu.VMEM((pools, halves, group_rows, query_width // halves), bf16),
+            pltpu.VMEM((pools, chips, CORES, rows_dev, w_out.shape[1]), bf16),
+            pltpu.VMEM((pools, chips, rows_dev, w_out.shape[1]), bf16),
+            pltpu.VMEM((pools, chips, rows_dev, w_out.shape[1]), bf16),
+            pltpu.VMEM((pools, chips, rows_dev, w_out.shape[1]), bf16),
+            pltpu.VMEM((pools, rows_dev, w_out.shape[1]), bf16),
+            pltpu.VMEM((pools, rows_dev, w_out.shape[1]), bf16),
+            dma(()),
+            dma((pools,)),
+            dma((pools,)),
+            dma((pools, halves)),
+            dma((pools, halves)),
+            dma((pools,)),
+            dma((pools,)),
+            dma((pools, chips)),
+            dma((pools, chips)),
+            dma((pools,)),
+            dma((pools,)),
+        ],
+        compiler_params=pltpu.CompilerParams(
+            collective_id=1, has_side_effects=True, vmem_limit_bytes=VMEM_BYTES
+        ),
+        name="output",
+    )(tokens, projected, fetched, cosine, sine, request_ids[:, None], key_request, placed_new, w_out)
+    return (mixed, stored.reshape(pools * CAPN, 1, PAGE * part))
+
+
 def solution(mesh):
+    whole_heads = mesh.shape["tp"] == KVH
     return jax.shard_map(
-        body,
+        fused if whole_heads else body,
         mesh=mesh,
         in_specs=(
             P(("pool", "tp"), None),

time: 468 us -> 123 us (0.26)
  waiting for transfers between devices: 382 us -> 0 us
  Pallas kernels: 0 us -> 111 us
  blocking collectives: 23.9 us -> 0 us
  matrix products: 18.6 us -> 0 us
  between operations: 14 us -> 0.7 us
  other arithmetic: 10.5 us -> 2.05 us
  starting transfers between devices: 8.41 us -> 0 us
    all_gather x2 -> x0, waiting for transfers between devices: 311 us -> none  [the longest x1 284 us: body(): full_out = lax.all_gather(w_out, 'pool', axis=1, tiled=True)]
    pallas_call x0 -> x2, Pallas kernels: none -> 111 us  [the longest x1 60.8 us: fused(): pl.pallas_call(functools.partial(output_kernel, pools, chips, heads, halv...]
    reduce_scatter x2 -> x0, waiting for transfers between devices: 36.3 us -> none  [the longest x1 29.3 us: body(): lax.psum_scatter(jnp.dot(attended, full_out, preferred_element_type=jnp.f...]
    all_to_all x2 -> x0, waiting for transfers between devices: 33.9 us -> none  [the longest x1 28.8 us: body(): lax.all_to_all(found, 'pool', split_axis=0, concat_axis=0, tiled=True)]
    all_to_all x2 -> x0, blocking collectives: 23.9 us -> none  [the longest x1 15.1 us: body(): lax.all_to_all(normed, 'pool', split_axis=1, concat_axis=0, tiled=True)]
    dot_general x6 -> x0, matrix products: 17.6 us -> none  [the longest x1 9.6 us: body(): jnp.dot(attended, full_out, preferred_element_type=jnp.float32)]
    all_to_all x2 -> x0, starting transfers between devices: 8.07 us -> none  [the longest x1 4.6 us: body(): lax.all_to_all(wanted, 'pool', split_axis=0, concat_axis=0, tiled=True)]
    gather x2 -> x0, local copies, waits for them, and re-layouts: 5.77 us -> none  [body(): found = jnp.take(pages_flat, asked.reshape(-1), axis=0)]
  transfers between devices with their start and end apart: 6 -> 0, of which waited for: 6 -> 0; matrix products, arithmetic and copies ran while one was open for 4% -> 0% of each run, Pallas kernels for 0% -> 0%
where the time goes in v1:
time: 123 us
  Pallas kernels  111 us (90%)
  local copies, waits for them, and re-layouts  9.25 us (8%)
  other arithmetic  2.05 us (2%)
    pallas_call x1, Pallas kernels, fused(): pl.pallas_call(functools.partial(output_kernel, pools, chips, heads, halv...  60.8 us
    pallas_call x1, Pallas kernels, fused(): pl.pallas_call(functools.partial(project_kernel, pools, chips, CAPF), out...  50.1 us

profile of v1, /device:TPU:0, one launch (start us, length us, event | category | flops | bytes accessed | tf_op | source)
XLA Modules:
  0.0 122.9 jit_solution(12128228385584585578)
XLA Ops:
  0.6 0.8 reshape.330
  1.4 0.2 convert_reduce_fusion
  1.6 0.1 select_reduce_fusion
  1.7 0.1 reshape.331
  1.8 0.6 pad.4.wanted_ref
  2.4 2.2 %reshape.332.keyval_ref = bf16[2048,256]{1,0:T(8,128)(2,1)} reshape(bf16[1024,512]{1,0:T(8,128)(2,1)} %param.13) | data formatting | bytes 2097152 | tf_op jit(solution)/shard_map/reshape | solution.py:533
  4.7 0.0 copy-start
  4.7 0.0 copy-start.1
  4.7 50.1 %project.1 = (f32[128,1280]{1,0:T(8,128)}, bf16[4,6,32,256]{3,2,1,0:T(8,128)(2,1)}) custom-call(bf16[16,8192]{1,0:T(8,128)(2,1)} %tokens_ref.3, s32[4,8,128]{2,1,0:T(8,128)} %pad.4.wanted_ref, bf16[2048,1024]{1,0:T(8,128)(2,1)} %query_ref.1, bf16[2048,256]{1,0:T(8,128)(2,1)} %reshape.332.keyval_ref, bf16[32,16,8192]{2,1,0:T(8,128)(2,1)} %bitcast.13), custom_call_target="tpu_custom_call" | custom-call | tf_op jit(solution)/shard_map/project/pallas_call | solution.py:567
  54.8 0.0 copy-done
  54.8 0.2 reduce-window.4
  55.0 0.1 convert_reduce_fusion.2
  55.1 0.1 select_reduce_fusion.2
  55.2 0.3 fusion
  55.5 0.8 pad_maximum_fusion
  56.2 0.1 broadcast_in_dim.67
  56.3 0.1 reshape.336
  56.4 0.6 broadcast_in_dim.68.key_request_ref
  57.0 0.7 copy.19.request_ref
  57.7 0.0 copy-done.1
  57.7 0.2 convert_reduce_fusion.1
  57.9 0.1 fusion.3
  58.0 0.6 reshape.338.placed_ref
  58.6 60.8 %output.1 = (f32[16,8192]{1,0:T(8,128)}, bf16[8,32,256]{2,1,0:T(8,128)(2,1)}) custom-call(bf16[16,8192]{1,0:T(8,128)(2,1)} %tokens_ref.3, f32[128,1280]{1,0:T(8,128)} %get-tuple-element.6.projected_ref, bf16[4,6,32,256]{3,2,1,0:T(8,128)(2,1)} %get-tuple-element.7.fetched_ref, f32[128,128]{1,0:T(8,128)} %get-tuple-element.20.cosine_ref, ...), custom_call_target="tpu_custom_call" | custom-call | tf_op jit(solution)/shard_map/output/pallas_call | solution.py:608
  119.4 1.6 %reshape.337 = bf16[8,1,8192]{2,0,1:T(8,128)(2,1)} reshape(bf16[8,32,256]{2,1,0:T(8,128)(2,1)} %get-tuple-element.9) | data formatting | bytes 262144 | tf_op jit(solution)/shard_map/reshape | solution.py:646
  121.0 1.9 %copy.21 = f32[16,8192]{1,0:T(8,128)} copy(f32[16,8192]{1,0:T(8,128)} %get-tuple-element.24) | data formatting | bytes 1048576
  (11 shorter events, 0.1 us)
Async XLA Ops:
  4.7 50.1 %copy-start = (s32[1,4]{1,0:T(1,128)S(1)}, s32[1,4]{1,0:T(1,128)}, u32[]{:S(2)}) copy-start(s32[1,4]{1,0:T(1,128)} %param.9) | copy-start | bytes 52
  4.7 53.1 %copy-start.1 = (s32[1,4]{1,0:T(1,128)S(1)}, s32[1,4]{1,0:T(1,128)}, u32[]{:S(2)}) copy-start(s32[1,4]{1,0:T(1,128)} %param.11) | copy-start | bytes 52
